TPU v7x, 32 devices: a whole 2x2x4 slice. The times are simulated.
32 devices in a mesh: pipe: 4 (over y, core), ctx: 4 (over z), tp: 2 (over x).
Axes of the slice: x: 2, y: 2, z: 4, core: 2. Of those that a mesh axis runs over, the one named last changes fastest.
Arguments:
- queries: bfloat16 [4, 512, 4096], P('pipe', 'ctx', 'tp'), may hold values from -15 to 15
- keys: bfloat16 [4, 512, 1024], P('pipe', 'ctx', 'tp'), may hold values from -5 to 5
- values: bfloat16 [4, 512, 1024], P('pipe', 'ctx', 'tp'), may hold values from -5 to 5
- span_ids: int32 [4, 8], P('pipe', 'ctx'), may hold values from 0 to 7, each once within a row
- cotangent: bfloat16 [4, 512, 4096], P('pipe', 'ctx'), may hold values from -6 to 6
Outputs:
- attention: bfloat16 [4, 512, 4096], P('pipe', 'ctx', 'tp')
- grad_out: bfloat16 [4, 4096, 4096], P('pipe', 'ctx', 'tp')
Inputs may be any that keep to these rules, and one draw needn't show every extreme that they name: `span_ids`: each row is a permutation of 0 to 7.
All inputs are finite; a program needn't handle non-finite values.
Results may differ from a plain program's by a relative error of at most 0.015.
Values may be sent and summed in bfloat16 or wider, within the bound.
No kernel may reach another device: no remote copies, remote signals or barrier semaphores. Data moves between devices by JAX's collectives and lax.ppermute only.
A program may use at most 64 MiB of HBM per device.

v0:
```python
import math

import jax
import jax.numpy as jnp
from jax import lax
from jax.sharding import PartitionSpec as P

HQ = 32
HK = 8
HD = 128


def from_partner(x, axis, apart):
    return lax.ppermute(x, axis, [(i, i ^ 1 << apart) for i in range(lax.axis_size(axis))])


def local(queries, keys, values, span_ids, cotangent):
    tokens = queries.shape[1]
    span = tokens // 2
    group = HQ // HK
    kv_heads = keys.shape[2] // HD
    scale = 1.0 / math.sqrt(HD)
    table = lax.all_gather(span_ids, "ctx", axis=1, tiled=True)[0]
    rows = jnp.arange(tokens, dtype=jnp.int32)
    query_pos = jnp.take(span_ids[0], rows // span) * span + rows % span
    query_heads = queries[0].reshape(tokens, kv_heads, group, HD).transpose(1, 2, 0, 3)
    start_top = jnp.full((kv_heads, group, tokens), -1e30, jnp.float32)
    top = start_top
    key_piece = lax.all_gather(keys, "ctx", axis=1, tiled=True)
    value_piece = lax.all_gather(values, "ctx", axis=1, tiled=True)
    count = key_piece.shape[1]
    key_block = key_piece[0].reshape(count, kv_heads, HD)
    value_block = value_piece[0].reshape(count, kv_heads, HD)
    scores = (
        jnp.einsum("kgtd,nkd->kgtn", query_heads, key_block, preferred_element_type=jnp.float32)
        * scale
    )
    key_rows = jnp.arange(count, dtype=jnp.int32)
    key_pos = jnp.take(table, key_rows // span) * span + key_rows % span
    visible = key_pos[None, :] <= query_pos[:, None]
    masked = jnp.where(visible, scores, -1e30)
    new_top = jnp.maximum(top, jnp.max(masked, axis=-1))
    weights = jnp.where(visible, jnp.exp(scores - new_top[..., None]), 0.0)
    total = jnp.sum(weights, axis=-1)
    mixed = jnp.einsum(
        "kgtn,nkd->kgtd",
        weights.astype(jnp.bfloat16),
        value_block,
        preferred_element_type=jnp.float32,
    )
    summed = mixed
    top, total, summed = (new_top, total, summed)
    output = (
        (summed / total[..., None]).transpose(2, 0, 1, 3).reshape(tokens, kv_heads * group * HD)
    )
    attention = output.astype(jnp.bfloat16)
    cot_rows = cotangent[0]
    cycle_size = lax.axis_size("ctx")
    moved = lax.all_to_all(cot_rows, "ctx", split_axis=1, concat_axis=0, tiled=True)
    everyone = lax.all_gather(attention, "ctx", axis=0, tiled=True)
    terms = jnp.einsum(
        "std,stc->sdc",
        moved.reshape(cycle_size, tokens, -1),
        everyone.reshape(cycle_size, tokens, -1),
        preferred_element_type=jnp.float32,
    )
    rounded = lax.optimization_barrier(terms.astype(jnp.bfloat16)).astype(jnp.float32)
    grad_share = jnp.sum(rounded, axis=0)
    top_bit = lax.axis_size("pipe").bit_length() - 2
    partner = from_partner(grad_share.astype(jnp.bfloat16), "pipe", top_bit).astype(
        grad_share.dtype
    )
    grad_out = (grad_share + partner).astype(jnp.bfloat16)
    return (attention[None], grad_out[None])


def solution(mesh):
    placed = (
        P("pipe", "ctx", "tp"),
        P("pipe", "ctx", "tp"),
        P("pipe", "ctx", "tp"),
        P("pipe", "ctx"),
        P("pipe", "ctx", None),
    )
    return jax.shard_map(
        local,
        mesh=mesh,
        in_specs=placed,
        out_specs=(P("pipe", "ctx", "tp"), P("pipe", "ctx", "tp")),
        check_vma=False,
    )
```

profile of v0, /device:TPU:0, one launch (start us, length us, event | category | flops | bytes accessed | tf_op | source)
XLA Modules:
  0.0 262.1 jit_solution(15832858932273261112)
XLA Ops:
  7.2 0.0 all-gather.2.cloned.1.call-start
  7.2 1.3 fusion.32
  8.5 1.2 dynamic-slice
  10.4 0.8 bitcast_dynamic-update-slice_fusion
  11.2 9.9 %all-reduce = s32[8]{0:T(128)S(1)} all-reduce(s32[8]{0:T(128)S(1)} %bitcast_dynamic-update-slice_fusion), channel_id=1, replica_groups=mesh['pipe'=4,'ctx'=4,'tp'=2] {'ctx'}, use_global_device_ids=true, to_apply=%add | all-reduce | flops 8 | bytes 64
  21.1 0.7 fusion.33
  21.8 1.0 copy.20
  22.9 13.9 %all_gather.13 = bf16[1,512,512]{1,2,0:T(8,128)(2,1)S(1)} all-gather(bf16[1,128,512]{1,2,0:T(8,128)(2,1)S(1)} %copy.20), channel_id=1, replica_groups=mesh['pipe'=4,'ctx'=4,'tp'=2] {'ctx'}, dimensions={1}, use_global_device_ids=true | all-gather | bytes 655360 | tf_op jit(solution)/shard_map/all_gather | solution.py:29
  36.8 1.4 reshape_squeeze.9
  38.2 15.1 %all_gather.14 = bf16[1,512,512]{2,1,0:T(8,128)(2,1)S(1)} all-gather(bf16[1,128,512]{2,1,0:T(8,128)(2,1)} %param.7), channel_id=1, replica_groups=mesh['pipe'=4,'ctx'=4,'tp'=2] {'ctx'}, dimensions={1}, use_global_device_ids=true | all-gather | bytes 655360 | tf_op jit(solution)/shard_map/all_gather | solution.py:30
  53.3 0.2 copy.22
  53.5 1.3 fusion.27
  54.8 4.4 %compare_select_fusion.1 = s32[512,1]{0,1:T(1,128)S(1)} fusion(s32[]{:T(128)} %bitcast.4, s32[]{:T(128)} %bitcast.5, s32[]{:T(128)} %bitcast.6, s32[]{:T(128)} %bitcast.7, s32[]{:T(128)} %bitcast.8, s32[]{:T(128)} %bitcast.10, s32[]{:T(128)} %bitcast.9), kind=kLoop, calls=%fused_computation.22 | loop fusion | flops 11776 | bytes 2076 | tf_op jit(solution)/shard_map/jit(_take)/gather | solution.py:39
  59.2 0.7 fusion.22
  59.9 0.1 broadcast_compare_fusion
  60.0 0.9 select_reduce_fusion
  60.9 1.2 fusion.1
  62.1 0.0 copy-start.1
  62.2 1.1 divide_convert_fusion
  63.3 1.0 copy.23
  64.3 0.0 all-gather.2.cloned.1.call-update
  64.3 0.0 copy-done.1
  64.3 0.7 copy.24
  65.0 0.5 copy.25
  65.5 48.5 %all_to_all.16 = bf16[128,4,1024]{2,0,1:T(8,128)(2,1)S(1)} all-to-all(bf16[128,4,1024]{2,0,1:T(8,128)(2,1)S(1)} %copy.25), channel_id=1, replica_groups=mesh['pipe'=4,'ctx'=4,'tp'=2] {'ctx'}, dimensions={1} | all-to-all | bytes 2097152 | tf_op jit(solution)/shard_map/all_to_all | solution.py:59
  114.0 9.7 %all-gather.2.cloned.1.call-done = bf16[512,2048]{1,0:T(8,128)(2,1)} async-done(((bf16[128,2048]{1,0:T(8,128)(2,1)}), bf16[512,2048]{1,0:T(8,128)(2,1)}) %all-gather.2.cloned.1.call-update) | async-done | bytes 2097168 | tf_op jit(solution)/shard_map/all_gather | solution.py:60
  123.7 9.9 %convert_bitcast_fusion = bf16[4,1024,2048]{1,2,0:T(8,128)(2,1)} fusion(bf16[4,128,2048]{2,1,0:T(8,128)(2,1)} %bitcast.57, bf16[128,4,1024]{2,0,1:T(8,128)(2,1)S(1)} %all_to_all.16), kind=kOutput, calls=%fused_computation.1 | convolution fusion | flops 2155872256 | bytes 19922944 | tf_op jit(solution)/shard_map/std,stc->sdc/dot_general | solution.py:61
  133.6 9.8 %convert_reduce_fusion = f32[1024,2048]{0,1:T(8,128)S(1)} fusion(bf16[4,1024,2048]{1,2,0:T(8,128)(2,1)} %convert_bitcast_fusion), kind=kLoop, calls=%fused_computation | loop fusion | flops 14680064 | bytes 25165824 | tf_op jit(solution)/shard_map/reduce_sum | solution.py:68
  143.4 0.0 copy-start
  143.4 3.1 %convert_element_type.44 = bf16[1024,2048]{0,1:T(8,128)(2,1)} convert(f32[1024,2048]{0,1:T(8,128)S(1)} %convert_reduce_fusion) | non-fusion elementwise | flops 2097152 | bytes 12582912 | tf_op jit(solution)/shard_map/convert_element_type | solution.py:70
  146.5 1.4 copy-done
  147.9 1.5 collective-permute-start
  149.4 1.0 copy.27
  150.4 90.3 %collective-permute-done = bf16[1024,2048]{0,1:T(8,128)(2,1)} collective-permute-done((bf16[1024,2048]{0,1:T(8,128)(2,1)}, bf16[1024,2048]{0,1:T(8,128)(2,1)}, u32[]{:S(2)}, u32[]{:S(2)}) %collective-permute-start) | collective-permute-done | bytes 4194336 | tf_op jit(solution)/shard_map/ppermute | solution.py:14
  240.7 8.1 %fusion = bf16[1,1024,2048]{1,2,0:T(8,128)(2,1)} fusion(f32[1024,2048]{0,1:T(8,128)} %copy-done, bf16[1024,2048]{0,1:T(8,128)(2,1)} %collective-permute-done), kind=kLoop, calls=%fused_computation.3 | loop fusion | flops 6291456 | bytes 16777216 | tf_op jit(solution)/shard_map/broadcast_in_dim | solution.py:74
  248.9 6.4 %copy.28 = bf16[1,1024,2048]{2,1,0:T(8,128)(2,1)} copy(bf16[1,1024,2048]{1,2,0:T(8,128)(2,1)} %fusion) | data formatting | bytes 8388608
  (3 shorter events, 0.0 us)
Async XLA Ops:
  7.2 116.6 %all-gather.2.cloned.1.call-start = ((), (), s32[]{:S(2)}) async-start(), calls=%async_computation.1 | async-start | bytes 2621440 | tf_op jit(solution)/shard_map/all_gather | solution.py:60
  62.1 2.2 copy-start.1
  143.4 4.5 %copy-start = (f32[1024,2048]{0,1:T(8,128)}, f32[1024,2048]{0,1:T(8,128)S(1)}, u32[]{:S(2)}) copy-start(f32[1024,2048]{0,1:T(8,128)S(1)} %convert_reduce_fusion) | copy-start | bytes 25165828
  147.9 92.8 %collective-permute-start = (bf16[1024,2048]{0,1:T(8,128)(2,1)}, bf16[1024,2048]{0,1:T(8,128)(2,1)}, u32[]{:S(2)}, u32[]{:S(2)}) collective-permute-start(bf16[1024,2048]{0,1:T(8,128)(2,1)} %convert_element_type.44), channel_id=1, source_target_pairs={{0,16},{8,24},{16,0},{24,8},{1,17},{9,25},{17,1},{25,9},{2,18},{10... | collective-permute-start | bytes 12582920 | tf_op jit(solution)/shard_map/ppermute | solution.py:14
Sparse Core Ops, SparseCore 0:
  64.4 59.2 all-gather.1
where the time goes:
time: 263 us; the launch traced here: 262 us
  waiting for transfers between devices  100 us (38%)
  blocking collectives  87.4 us (33%)
  other arithmetic  28.7 us (11%)
  local copies, waits for them, and re-layouts  17.7 us (7%)
  between operations  14.8 us (6%)
  matrix products  11.9 us (5%)
    ppermute x1, waiting for transfers between devices, from_partner(): lax.ppermute(x, axis, [(i, i ^ 1 << apart) for i in range(lax.axis_size(a...  90.3 us
    all_to_all x1, blocking collectives, local(): lax.all_to_all(cot_rows, 'ctx', split_axis=1, concat_axis=0, tiled=True)  48.5 us
    all_gather x1, blocking collectives, local(): value_piece = lax.all_gather(values, 'ctx', axis=1, tiled=True)  15.1 us
    all_gather x1, blocking collectives, local(): key_piece = lax.all_gather(keys, 'ctx', axis=1, tiled=True)  13.9 us
    unnamed x11, local copies, waits for them, and re-layouts  12.5 us
    unnamed x1, blocking collectives  9.91 us
    dot_general x1, matrix products, local(): jnp.einsum('std,stc->sdc', moved.reshape(cycle_size, tokens, -1), everyon...  9.87 us
    reduce_sum x1, other arithmetic, local(): grad_share = jnp.sum(rounded, axis=0)  9.83 us
  transfers between devices with their start and end apart: 2, of which 2 were waited for; matrix products, arithmetic and copies ran while one was open for 1% of the time, Pallas kernels for 0%

commit v1 on v0

v1 whole, which is shorter than its diff:
```python
import functools
import math

import jax
import jax.numpy as jnp
from jax import lax
from jax.experimental import pallas as pl
from jax.experimental.pallas import tpu as pltpu
from jax.sharding import PartitionSpec as P

HQ = 32
HK = 8
HD = 128
TAG = 16
VMEM = pl.BlockSpec(memory_space=pltpu.VMEM)
SMEM = pl.BlockSpec(memory_space=pltpu.SMEM)


def swap(x, axis, mask):
    return lax.ppermute(x, axis, [(i, i ^ mask) for i in range(lax.axis_size(axis))])


def params(mib):
    return pltpu.CompilerParams(vmem_limit_bytes=mib * 2**20)


def pack_kernel(n, span_ref, key_ref, value_ref, cot_ref, packed_ref, *cot_refs):
    tokens, width = key_ref.shape[1:]
    spans = span_ref.shape[1]
    packed_ref[:tokens, :width] = key_ref[0]
    packed_ref[:tokens, width:] = value_ref[0]
    lane = lax.broadcasted_iota(jnp.int32, (TAG, 2 * width), 1)
    ids = jnp.zeros((TAG, 2 * width), jnp.float32)
    for j in range(spans):
        ids = jnp.where(lane // (tokens // spans) == j, span_ref[0, j].astype(jnp.float32), ids)
    packed_ref[tokens:, :] = ids.astype(jnp.bfloat16)
    me = lax.axis_index("ctx")
    side = lax.axis_index("tp") & 1
    half = cot_ref.shape[2] // n // 2
    for s in range(n):
        at = pl.multiple_of((jnp.bitwise_xor(me, s) * 2 + side) * half, 128)
        cot_refs[s][...] = cot_ref[0, :, pl.ds(at, half)]


def attention_kernel(group, scale, span_ref, query_ref, *refs):
    kv_refs, out_ref = refs[:-1], refs[-1]
    tokens = query_ref.shape[1]
    width = kv_refs[0].shape[1] // 2
    spans = span_ref.shape[1]
    span = tokens // spans
    lane = lax.broadcasted_iota(jnp.int32, (1, tokens), 1)
    inner = (lane % span).astype(jnp.float32)
    key_pos = jnp.concatenate(
        [ref[tokens : tokens + 1, :tokens].astype(jnp.float32) * span + inner for ref in kv_refs],
        axis=1,
    )
    row = lax.broadcasted_iota(jnp.int32, (tokens, 1), 0)
    base = jnp.zeros((tokens, 1), jnp.int32)
    for j in range(spans):
        base = jnp.where(row // span == j, span_ref[0, j] * span, base)
    query_pos = (base + row % span).astype(jnp.float32)
    hidden = jnp.where(key_pos <= query_pos, 0.0, -1e30)
    hidden = jnp.concatenate([hidden] * group, axis=0)
    for j in range(width // HD):
        columns = slice(j * HD, (j + 1) * HD)
        key_block = jnp.concatenate([ref[:tokens, columns] for ref in kv_refs], axis=0)
        value_block = jnp.concatenate(
            [ref[:tokens, width + j * HD : width + (j + 1) * HD] for ref in kv_refs], axis=0
        )
        queries = jnp.concatenate(
            [query_ref[0, :, (j * group + g) * HD : (j * group + g + 1) * HD] for g in range(group)],
            axis=0,
        )
        scores = lax.dot_general(
            queries, key_block, (((1,), (1,)), ((), ())), preferred_element_type=jnp.float32
        )
        scores = jnp.where(hidden < 0.0, hidden, scores)
        top = jnp.max(scores, axis=1, keepdims=True)
        weights = jnp.exp2((scores - top) * (scale * math.log2(math.e)))
        total = jnp.sum(weights, axis=1, keepdims=True)
        mixed = jnp.dot(
            weights.astype(jnp.bfloat16), value_block, preferred_element_type=jnp.float32
        )
        mixed = (mixed / total).astype(jnp.bfloat16)
        for g in range(group):
            out_ref[0, :, (j * group + g) * HD : (j * group + g + 1) * HD] = mixed[
                g * tokens : (g + 1) * tokens
            ]


def turn_kernel(*refs):
    tokens = refs[0].shape[0]
    for s, ref in enumerate(refs[:-1]):
        refs[-1][:, s * tokens : (s + 1) * tokens] = ref[...].T


def grad_kernel(n, *refs):
    att_refs, (own_ref, own_far_ref, near_ref, far_ref), out_ref = refs[: 2 * n], refs[2 * n : -1], refs[-1]
    rows = jnp.concatenate([ref[0] for ref in att_refs], axis=0)
    depth = rows.shape[0] // 2
    half = own_ref.shape[0]
    side = lax.axis_index("tp") & 1
    for at, (left, right) in (
        (side, (own_ref, own_far_ref)),
        (1 - side, (near_ref, far_ref)),
    ):
        both = jnp.concatenate([left[...], right[...]], axis=1)
        out_ref[0, pl.ds(pl.multiple_of(at * half, half), half), :] = jnp.dot(
            both, rows, preferred_element_type=jnp.float32
        ).astype(jnp.bfloat16)


def local(queries, keys, values, span_ids, cotangent):
    n = lax.axis_size("ctx")
    far = lax.axis_size("pipe") // 2
    tokens, width = keys.shape[1:]
    heads = queries.shape[2]
    features = cotangent.shape[2] // n
    half = features // 2
    packed, *cots = pl.pallas_call(
        functools.partial(pack_kernel, n),
        out_shape=[jax.ShapeDtypeStruct((tokens + TAG, 2 * width), jnp.bfloat16)]
        + [jax.ShapeDtypeStruct((tokens, half), jnp.bfloat16)] * n,
        in_specs=[SMEM, VMEM, VMEM, VMEM],
        out_specs=[VMEM] * (n + 1),
        compiler_params=params(16),
        name="pack",
    )(span_ids, keys, values, cotangent)
    kv = [packed] + [swap(packed, "ctx", s) for s in range(1, n)]
    cots = cots[:1] + [swap(cots[s], "ctx", s) for s in range(1, n)]
    attention = pl.pallas_call(
        functools.partial(attention_kernel, HQ // HK, 1.0 / math.sqrt(HD)),
        out_shape=jax.ShapeDtypeStruct(queries.shape, jnp.bfloat16),
        in_specs=[SMEM] + [VMEM] * (n + 1),
        out_specs=VMEM,
        compiler_params=params(40),
        name="attend",
    )(span_ids, queries, *kv)
    near = [attention] + [swap(attention, "ctx", s) for s in range(1, n)]
    turned = pl.pallas_call(
        turn_kernel,
        out_shape=jax.ShapeDtypeStruct((half, n * tokens), jnp.bfloat16),
        in_specs=[VMEM] * n,
        out_specs=VMEM,
        compiler_params=params(16),
        name="turn",
    )(*cots)
    turned_far = swap(turned, "pipe", far)
    other = swap(turned, "tp", 1)
    other_far = swap(turned_far, "tp", 1)
    mirrored = [swap(piece, "pipe", far) for piece in near]
    tile = min(256, heads)
    piece_spec = pl.BlockSpec((1, tokens, tile), lambda j: (0, 0, j))
    grad_out = pl.pallas_call(
        functools.partial(grad_kernel, n),
        grid=(heads // tile,),
        out_shape=jax.ShapeDtypeStruct((1, features, heads), jnp.bfloat16),
        in_specs=[piece_spec] * (2 * n)
        + [pl.BlockSpec((half, n * tokens), lambda j: (0, 0))] * 4,
        out_specs=pl.BlockSpec((1, features, tile), lambda j: (0, 0, j)),
        compiler_params=params(40),
        cost_estimate=pl.CostEstimate(
            flops=4 * features * heads * n * tokens, bytes_accessed=12 * 2**20, transcendentals=0
        ),
        name="gradient",
    )(*near, *mirrored, turned, turned_far, other, other_far)
    return (attention, grad_out)


def solution(mesh):
    placed = (
        P("pipe", "ctx", "tp"),
        P("pipe", "ctx", "tp"),
        P("pipe", "ctx", "tp"),
        P("pipe", "ctx"),
        P("pipe", "ctx", None),
    )
    return jax.shard_map(
        local,
        mesh=mesh,
        in_specs=placed,
        out_specs=(P("pipe", "ctx", "tp"), P("pipe", "ctx", "tp")),
        check_vma=False,
    )
```

time: 263 us -> 134 us (0.51)
  blocking collectives: 87.4 us -> 0 us
  other arithmetic: 28.7 us -> 0 us
  starting transfers between devices: 1.56 us -> 22.6 us
  between operations: 14.8 us -> 0.69 us
  matrix products: 11.9 us -> 0 us
  local copies, waits for them, and re-layouts: 17.7 us -> 6.41 us
  Pallas kernels: 0 us -> 11.1 us
  waiting for transfers between devices: 100 us -> 92.4 us
    all_to_all x1 -> x0, blocking collectives: 48.5 us -> none  [local(): lax.all_to_all(cot_rows, 'ctx', split_axis=1, concat_axis=0, tiled=True)]
    all_gather x2 -> x0, blocking collectives: 29.1 us -> none  [the longest x1 15.1 us: local(): value_piece = lax.all_gather(values, 'ctx', axis=1, tiled=True)]
    ppermute x1 -> x16, starting transfers between devices: 1.52 us -> 22.6 us  [swap(): lax.ppermute(x, axis, [(i, i ^ mask) for i in range(lax.axis_size(axis))])]
    dot_general x3 -> x0, matrix products: 11.9 us -> none  [the longest x1 9.87 us: local(): jnp.einsum('std,stc->sdc', moved.reshape(cycle_size, tokens, -1), everyon...]
    pallas_call x0 -> x4, Pallas kernels: none -> 11.1 us  [the longest x1 7.34 us: local(): pl.pallas_call(functools.partial(grad_kernel, n), grid=(heads // tile,),...]
    reduce_sum x2 -> x0, other arithmetic: 11 us -> none  [the longest x1 9.83 us: local(): grad_share = jnp.sum(rounded, axis=0)]
    unnamed x1 -> x0, blocking collectives: 9.91 us -> none
    all_gather x1 -> x0, waiting for transfers between devices: 9.74 us -> none  [local(): everyone = lax.all_gather(attention, 'ctx', axis=0, tiled=True)]
  transfers between devices with their start and end apart: 2 -> 16, of which waited for: 2 -> 7; matrix products, arithmetic and copies ran while one was open for 1% -> 0% of each run, Pallas kernels for 0% -> 2%
where the time goes in v1:
time: 134 us; the launch traced here: 133 us
  waiting for transfers between devices  92.4 us (69%)
  starting transfers between devices  22.6 us (17%)
  Pallas kernels  11.1 us (8%)
  local copies, waits for them, and re-layouts  6.41 us (5%)
    ppermute x16, waiting for transfers between devices, swap(): lax.ppermute(x, axis, [(i, i ^ mask) for i in range(lax.axis_size(axis))])  92.4 us
    ppermute x16, starting transfers between devices, swap(): lax.ppermute(x, axis, [(i, i ^ mask) for i in range(lax.axis_size(axis))])  22.6 us
    pallas_call x1, Pallas kernels, local(): pl.pallas_call(functools.partial(grad_kernel, n), grid=(heads // tile,),...  7.34 us
    unnamed x14, local copies, waits for them, and re-layouts  6.41 us
    pallas_call x1, Pallas kernels, local(): pl.pallas_call(functools.partial(attention_kernel, HQ // HK, 1.0 / math.s...  3.03 us
  transfers between devices with their start and end apart: 16, of which 7 were waited for; matrix products, arithmetic and copies ran while one was open for 0% of the time, Pallas kernels for 2%

profile of v1, /device:TPU:0, one launch (start us, length us, event | category | flops | bytes accessed | tf_op | source)
XLA Modules:
  0.0 133.2 jit_solution(13920085414851201454)
XLA Ops:
  0.6 0.0 copy-start
  0.6 1.2 copy-done
  1.9 0.0 copy-start.3
  1.9 0.9 copy-done.3
  2.8 0.0 copy-start.4
  2.8 0.9 copy-done.4
  3.7 0.0 copy-start.5
  3.7 0.7 copy-done.5
  4.3 0.6 pack.1
  4.9 5.1 %collective-permute-start.2 = (bf16[144,1024]{1,0:T(8,128)(2,1)S(1)}, bf16[144,1024]{1,0:T(8,128)(2,1)S(1)}, u32[]{:S(2)}, u32[]{:S(2)}) collective-permute-start(bf16[144,1024]{1,0:T(8,128)(2,1)S(1)} %get-tuple-element.7.refs_0_), channel_id=1, source_target_pairs={{0,6},{2,4},{4,2},{6,0},{1,7},{3,5},{5,3},{7,1},{8,14},{10,12},{12... | collective-permute-start | bytes 884744 | tf_op jit(solution)/shard_map/ppermute | solution.py:20
  10.0 0.0 collective-permute-start.1
  10.0 0.6 collective-permute-start
  10.7 1.4 %collective-permute-start.10 = (bf16[128,512]{1,0:T(8,128)(2,1)S(1)}, bf16[128,512]{1,0:T(8,128)(2,1)S(1)}, u32[]{:S(2)}, u32[]{:S(2)}) collective-permute-start(bf16[128,512]{1,0:T(8,128)(2,1)S(1)} %get-tuple-element.9), channel_id=1, source_target_pairs={{0,2},{2,0},{4,6},{6,4},{1,3},{3,1},{5,7},{7,5},{8,10},{10,8},{12,... | collective-permute-start | bytes 393224 | tf_op jit(solution)/shard_map/ppermute | solution.py:20
  12.1 2.9 %collective-permute-start.11 = (bf16[128,512]{1,0:T(8,128)(2,1)S(1)}, bf16[128,512]{1,0:T(8,128)(2,1)S(1)}, u32[]{:S(2)}, u32[]{:S(2)}) collective-permute-start(bf16[128,512]{1,0:T(8,128)(2,1)S(1)} %get-tuple-element.10), channel_id=1, source_target_pairs={{0,4},{2,6},{4,0},{6,2},{1,5},{3,7},{5,1},{7,3},{8,12},{10,14},{12... | collective-permute-start | bytes 393224 | tf_op jit(solution)/shard_map/ppermute | solution.py:20
  15.0 18.0 %collective-permute-done.10.refs_1_ = bf16[128,512]{1,0:T(8,128)(2,1)S(1)} collective-permute-done((bf16[128,512]{1,0:T(8,128)(2,1)S(1)}, bf16[128,512]{1,0:T(8,128)(2,1)S(1)}, u32[]{:S(2)}, u32[]{:S(2)}) %collective-permute-start.10) | collective-permute-done | bytes 131104 | tf_op jit(solution)/shard_map/ppermute | solution.py:20
  32.9 0.0 collective-permute-start.12
  33.0 11.6 %collective-permute-done.11.refs_2_ = bf16[128,512]{1,0:T(8,128)(2,1)S(1)} collective-permute-done((bf16[128,512]{1,0:T(8,128)(2,1)S(1)}, bf16[128,512]{1,0:T(8,128)(2,1)S(1)}, u32[]{:S(2)}, u32[]{:S(2)}) %collective-permute-start.11) | collective-permute-done | bytes 131104 | tf_op jit(solution)/shard_map/ppermute | solution.py:20
  44.5 0.0 collective-permute-done.12.refs_3_
  44.5 0.2 turn.1.refs_8_
  44.7 1.6 %collective-permute-start.14 = (bf16[512,512]{1,0:T(8,128)(2,1)S(1)}, bf16[512,512]{1,0:T(8,128)(2,1)S(1)}, u32[]{:S(2)}, u32[]{:S(2)}) collective-permute-start(bf16[512,512]{1,0:T(8,128)(2,1)S(1)} %turn.1.refs_8_), channel_id=1, source_target_pairs={{0,1},{1,0},{2,3},{3,2},{4,5},{5,4},{6,7},{7,6},{8,9},{9,8},{10,11... | collective-permute-start | bytes 1572872 | tf_op jit(solution)/shard_map/ppermute | solution.py:20
  46.3 1.5 %collective-permute-start.13 = (bf16[512,512]{1,0:T(8,128)(2,1)S(1)}, bf16[512,512]{1,0:T(8,128)(2,1)S(1)}, u32[]{:S(2)}, u32[]{:S(2)}) collective-permute-start(bf16[512,512]{1,0:T(8,128)(2,1)S(1)} %turn.1.refs_8_), channel_id=1, source_target_pairs={{0,16},{8,24},{16,0},{24,8},{1,17},{9,25},{17,1},{25,9},{2,18},{10... | collective-permute-start | bytes 1572872 | tf_op jit(solution)/shard_map/ppermute | solution.py:20
  47.8 0.0 collective-permute-done.2.refs_3_
  47.8 0.0 collective-permute-done.1.refs_2_
  47.8 0.0 collective-permute-done.refs_1_
  47.8 0.0 copy-start.1
  47.8 1.0 copy-done.1
  48.9 0.7 copy-done.6
  49.5 3.0 %attend.1.refs_0_ = bf16[1,128,2048]{2,1,0:T(8,128)(2,1)} custom-call(s32[1,2]{1,0:T(1,128)S(1)} %copy-done.6, bf16[1,128,2048]{2,1,0:T(8,128)(2,1)S(1)} %copy-done.1, bf16[144,1024]{1,0:T(8,128)(2,1)S(1)} %get-tuple-element.7.refs_0_, bf16[144,1024]{1,0:T(8,128)(2,1)S(1)} %collective-permute-done.refs_1_, ...), custom_call_target="tpu_custom_call" | custom-call | tf_op jit(solution)/shard_map/attend/pallas_call | solution.py:131
  52.6 2.7 %collective-permute-start.5 = (bf16[1,128,2048]{2,1,0:T(8,128)(2,1)}, bf16[1,128,2048]{2,1,0:T(8,128)(2,1)S(1)}, u32[]{:S(2)}, u32[]{:S(2)}) collective-permute-start(bf16[1,128,2048]{2,1,0:T(8,128)(2,1)} %attend.1.refs_0_), channel_id=1, source_target_pairs={{0,6},{2,4},{4,2},{6,0},{1,7},{3,5},{5,3},{7,1},{8,14},{10,12},{12... | collective-permute-start | bytes 1572872 | tf_op jit(solution)/shard_map/ppermute | solution.py:20
  55.2 1.2 collective-permute-start.4
  56.4 0.5 collective-permute-start.3
  57.0 0.0 collective-permute-done.14.refs_10_
  57.0 1.4 %collective-permute-start.6 = (bf16[1,128,2048]{2,1,0:T(8,128)(2,1)}, bf16[1,128,2048]{2,1,0:T(8,128)(2,1)S(1)}, u32[]{:S(2)}, u32[]{:S(2)}) collective-permute-start(bf16[1,128,2048]{2,1,0:T(8,128)(2,1)} %attend.1.refs_0_), channel_id=1, source_target_pairs={{0,16},{8,24},{16,0},{24,8},{1,17},{9,25},{17,1},{25,9},{2,18},{10... | collective-permute-start | bytes 1572872 | tf_op jit(solution)/shard_map/ppermute | solution.py:20
  58.3 0.4 collective-permute-done.13.refs_9_
  58.7 1.1 collective-permute-start.15
  59.8 9.7 %collective-permute-done.5.refs_3_ = bf16[1,128,2048]{2,1,0:T(8,128)(2,1)S(1)} collective-permute-done((bf16[1,128,2048]{2,1,0:T(8,128)(2,1)}, bf16[1,128,2048]{2,1,0:T(8,128)(2,1)S(1)}, u32[]{:S(2)}, u32[]{:S(2)}) %collective-permute-start.5) | collective-permute-done | bytes 524320 | tf_op jit(solution)/shard_map/ppermute | solution.py:20
  69.5 0.5 collective-permute-start.9
  70.0 29.7 %collective-permute-done.4.refs_2_ = bf16[1,128,2048]{2,1,0:T(8,128)(2,1)S(1)} collective-permute-done((bf16[1,128,2048]{2,1,0:T(8,128)(2,1)}, bf16[1,128,2048]{2,1,0:T(8,128)(2,1)S(1)}, u32[]{:S(2)}, u32[]{:S(2)}) %collective-permute-start.4) | collective-permute-done | bytes 524320 | tf_op jit(solution)/shard_map/ppermute | solution.py:20
  99.7 0.5 collective-permute-start.8
  100.2 0.0 collective-permute-done.3.refs_1_
  100.2 1.5 %collective-permute-start.7 = (bf16[1,128,2048]{2,1,0:T(8,128)(2,1)S(1)}, bf16[1,128,2048]{2,1,0:T(8,128)(2,1)S(1)}, u32[]{:S(2)}, u32[]{:S(2)}) collective-permute-start(bf16[1,128,2048]{2,1,0:T(8,128)(2,1)S(1)} %collective-permute-done.3.refs_1_), channel_id=1, source_target_pairs={{0,16},{8,24},{16,0},{24,8},{1,17},{9,25},{17,1},{25,9},{2,18},{10... | collective-permute-start | bytes 1572872 | tf_op jit(solution)/shard_map/ppermute | solution.py:20
  101.8 0.0 collective-permute-done.6.refs_4_
  101.8 0.0 collective-permute-done.15.refs_11_
  101.8 0.0 collective-permute-done.9.refs_7_
  101.8 12.7 %collective-permute-done.8.refs_6_ = bf16[1,128,2048]{2,1,0:T(8,128)(2,1)S(1)} collective-permute-done((bf16[1,128,2048]{2,1,0:T(8,128)(2,1)S(1)}, bf16[1,128,2048]{2,1,0:T(8,128)(2,1)S(1)}, u32[]{:S(2)}, u32[]{:S(2)}) %collective-permute-start.8) | collective-permute-done | bytes 524320 | tf_op jit(solution)/shard_map/ppermute | solution.py:20
  114.5 10.3 %collective-permute-done.7.refs_5_ = bf16[1,128,2048]{2,1,0:T(8,128)(2,1)S(1)} collective-permute-done((bf16[1,128,2048]{2,1,0:T(8,128)(2,1)S(1)}, bf16[1,128,2048]{2,1,0:T(8,128)(2,1)S(1)}, u32[]{:S(2)}, u32[]{:S(2)}) %collective-permute-start.7) | collective-permute-done | bytes 524320 | tf_op jit(solution)/shard_map/ppermute | solution.py:20
  124.8 1.0 copy-done.2
  125.9 7.3 %gradient.1 = bf16[1,1024,2048]{2,1,0:T(8,128)(2,1)} custom-call(bf16[1,128,2048]{2,1,0:T(8,128)(2,1)S(1)} %copy-done.2, bf16[1,128,2048]{2,1,0:T(8,128)(2,1)S(1)} %collective-permute-done.3.refs_1_, bf16[1,128,2048]{2,1,0:T(8,128)(2,1)S(1)} %collective-permute-done.4.refs_2_, bf16[1,128,2048]{2,1,0:T(8,128)(2,1)S(1)} %collective-permute-done.5.refs_3_, ...), custom_call_target="tpu_custom_call" | custom-call | flops 4294967296 | bytes 12582912 | tf_op jit(solution)/shard_map/gradient/pallas_call | solution.py:154
  (2 shorter events, 0.0 us)
Async XLA Ops:
  0.6 1.2 copy-start
  1.9 0.9 copy-start.3
  2.8 0.9 copy-start.4
  3.7 0.7 copy-start.5
  4.9 42.9 %collective-permute-start.2 = (bf16[144,1024]{1,0:T(8,128)(2,1)S(1)}, bf16[144,1024]{1,0:T(8,128)(2,1)S(1)}, u32[]{:S(2)}, u32[]{:S(2)}) collective-permute-start(bf16[144,1024]{1,0:T(8,128)(2,1)S(1)} %get-tuple-element.7.refs_0_), channel_id=1, source_target_pairs={{0,6},{2,4},{4,2},{6,0},{1,7},{3,5},{5,3},{7,1},{8,14},{10,12},{12... | collective-permute-start | bytes 884744 | tf_op jit(solution)/shard_map/ppermute | solution.py:20
  10.0 37.8 %collective-permute-start.1 = (bf16[144,1024]{1,0:T(8,128)(2,1)S(1)}, bf16[144,1024]{1,0:T(8,128)(2,1)S(1)}, u32[]{:S(2)}, u32[]{:S(2)}) collective-permute-start(bf16[144,1024]{1,0:T(8,128)(2,1)S(1)} %get-tuple-element.7.refs_0_), channel_id=1, source_target_pairs={{0,4},{2,6},{4,0},{6,2},{1,5},{3,7},{5,1},{7,3},{8,12},{10,14},{12... | collective-permute-start | bytes 884744 | tf_op jit(solution)/shard_map/ppermute | solution.py:20
  10.0 37.8 %collective-permute-start = (bf16[144,1024]{1,0:T(8,128)(2,1)S(1)}, bf16[144,1024]{1,0:T(8,128)(2,1)S(1)}, u32[]{:S(2)}, u32[]{:S(2)}) collective-permute-start(bf16[144,1024]{1,0:T(8,128)(2,1)S(1)} %get-tuple-element.7.refs_0_), channel_id=1, source_target_pairs={{0,2},{2,0},{4,6},{6,4},{1,3},{3,1},{5,7},{7,5},{8,10},{10,8},{12,... | collective-permute-start | bytes 884744 | tf_op jit(solution)/shard_map/ppermute | solution.py:20
  10.7 22.3 %collective-permute-start.10 = (bf16[128,512]{1,0:T(8,128)(2,1)S(1)}, bf16[128,512]{1,0:T(8,128)(2,1)S(1)}, u32[]{:S(2)}, u32[]{:S(2)}) collective-permute-start(bf16[128,512]{1,0:T(8,128)(2,1)S(1)} %get-tuple-element.9), channel_id=1, source_target_pairs={{0,2},{2,0},{4,6},{6,4},{1,3},{3,1},{5,7},{7,5},{8,10},{10,8},{12,... | collective-permute-start | bytes 393224 | tf_op jit(solution)/shard_map/ppermute | solution.py:20
  12.1 32.5 %collective-permute-start.11 = (bf16[128,512]{1,0:T(8,128)(2,1)S(1)}, bf16[128,512]{1,0:T(8,128)(2,1)S(1)}, u32[]{:S(2)}, u32[]{:S(2)}) collective-permute-start(bf16[128,512]{1,0:T(8,128)(2,1)S(1)} %get-tuple-element.10), channel_id=1, source_target_pairs={{0,4},{2,6},{4,0},{6,2},{1,5},{3,7},{5,1},{7,3},{8,12},{10,14},{12... | collective-permute-start | bytes 393224 | tf_op jit(solution)/shard_map/ppermute | solution.py:20
  32.9 11.6 %collective-permute-start.12 = (bf16[128,512]{1,0:T(8,128)(2,1)S(1)}, bf16[128,512]{1,0:T(8,128)(2,1)S(1)}, u32[]{:S(2)}, u32[]{:S(2)}) collective-permute-start(bf16[128,512]{1,0:T(8,128)(2,1)S(1)} %get-tuple-element.11), channel_id=1, source_target_pairs={{0,6},{2,4},{4,2},{6,0},{1,7},{3,5},{5,3},{7,1},{8,14},{10,12},{12... | collective-permute-start | bytes 393224 | tf_op jit(solution)/shard_map/ppermute | solution.py:20
  44.7 12.2 %collective-permute-start.14 = (bf16[512,512]{1,0:T(8,128)(2,1)S(1)}, bf16[512,512]{1,0:T(8,128)(2,1)S(1)}, u32[]{:S(2)}, u32[]{:S(2)}) collective-permute-start(bf16[512,512]{1,0:T(8,128)(2,1)S(1)} %turn.1.refs_8_), channel_id=1, source_target_pairs={{0,1},{1,0},{2,3},{3,2},{4,5},{5,4},{6,7},{7,6},{8,9},{9,8},{10,11... | collective-permute-start | bytes 1572872 | tf_op jit(solution)/shard_map/ppermute | solution.py:20
  46.3 12.4 %collective-permute-start.13 = (bf16[512,512]{1,0:T(8,128)(2,1)S(1)}, bf16[512,512]{1,0:T(8,128)(2,1)S(1)}, u32[]{:S(2)}, u32[]{:S(2)}) collective-permute-start(bf16[512,512]{1,0:T(8,128)(2,1)S(1)} %turn.1.refs_8_), channel_id=1, source_target_pairs={{0,16},{8,24},{16,0},{24,8},{1,17},{9,25},{17,1},{25,9},{2,18},{10... | collective-permute-start | bytes 1572872 | tf_op jit(solution)/shard_map/ppermute | solution.py:20
  47.8 1.0 copy-start.1
  48.9 0.7 copy-start.6
  52.6 17.0 %collective-permute-start.5 = (bf16[1,128,2048]{2,1,0:T(8,128)(2,1)}, bf16[1,128,2048]{2,1,0:T(8,128)(2,1)S(1)}, u32[]{:S(2)}, u32[]{:S(2)}) collective-permute-start(bf16[1,128,2048]{2,1,0:T(8,128)(2,1)} %attend.1.refs_0_), channel_id=1, source_target_pairs={{0,6},{2,4},{4,2},{6,0},{1,7},{3,5},{5,3},{7,1},{8,14},{10,12},{12... | collective-permute-start | bytes 1572872 | tf_op jit(solution)/shard_map/ppermute | solution.py:20
  55.2 44.5 %collective-permute-start.4 = (bf16[1,128,2048]{2,1,0:T(8,128)(2,1)}, bf16[1,128,2048]{2,1,0:T(8,128)(2,1)S(1)}, u32[]{:S(2)}, u32[]{:S(2)}) collective-permute-start(bf16[1,128,2048]{2,1,0:T(8,128)(2,1)} %attend.1.refs_0_), channel_id=1, source_target_pairs={{0,4},{2,6},{4,0},{6,2},{1,5},{3,7},{5,1},{7,3},{8,12},{10,14},{12... | collective-permute-start | bytes 1572872 | tf_op jit(solution)/shard_map/ppermute | solution.py:20
  56.4 43.8 %collective-permute-start.3 = (bf16[1,128,2048]{2,1,0:T(8,128)(2,1)}, bf16[1,128,2048]{2,1,0:T(8,128)(2,1)S(1)}, u32[]{:S(2)}, u32[]{:S(2)}) collective-permute-start(bf16[1,128,2048]{2,1,0:T(8,128)(2,1)} %attend.1.refs_0_), channel_id=1, source_target_pairs={{0,2},{2,0},{4,6},{6,4},{1,3},{3,1},{5,7},{7,5},{8,10},{10,8},{12,... | collective-permute-start | bytes 1572872 | tf_op jit(solution)/shard_map/ppermute | solution.py:20
  57.0 44.8 %collective-permute-start.6 = (bf16[1,128,2048]{2,1,0:T(8,128)(2,1)}, bf16[1,128,2048]{2,1,0:T(8,128)(2,1)S(1)}, u32[]{:S(2)}, u32[]{:S(2)}) collective-permute-start(bf16[1,128,2048]{2,1,0:T(8,128)(2,1)} %attend.1.refs_0_), channel_id=1, source_target_pairs={{0,16},{8,24},{16,0},{24,8},{1,17},{9,25},{17,1},{25,9},{2,18},{10... | collective-permute-start | bytes 1572872 | tf_op jit(solution)/shard_map/ppermute | solution.py:20
  58.7 43.0 %collective-permute-start.15 = (bf16[512,512]{1,0:T(8,128)(2,1)S(1)}, bf16[512,512]{1,0:T(8,128)(2,1)S(1)}, u32[]{:S(2)}, u32[]{:S(2)}) collective-permute-start(bf16[512,512]{1,0:T(8,128)(2,1)S(1)} %collective-permute-done.13.refs_9_), channel_id=1, source_target_pairs={{0,1},{1,0},{2,3},{3,2},{4,5},{5,4},{6,7},{7,6},{8,9},{9,8},{10,11... | collective-permute-start | bytes 1572872 | tf_op jit(solution)/shard_map/ppermute | solution.py:20
  69.5 32.2 %collective-permute-start.9 = (bf16[1,128,2048]{2,1,0:T(8,128)(2,1)S(1)}, bf16[1,128,2048]{2,1,0:T(8,128)(2,1)S(1)}, u32[]{:S(2)}, u32[]{:S(2)}) collective-permute-start(bf16[1,128,2048]{2,1,0:T(8,128)(2,1)S(1)} %collective-permute-done.5.refs_3_), channel_id=1, source_target_pairs={{0,16},{8,24},{16,0},{24,8},{1,17},{9,25},{17,1},{25,9},{2,18},{10... | collective-permute-start | bytes 1572872 | tf_op jit(solution)/shard_map/ppermute | solution.py:20
  99.7 14.8 %collective-permute-start.8 = (bf16[1,128,2048]{2,1,0:T(8,128)(2,1)S(1)}, bf16[1,128,2048]{2,1,0:T(8,128)(2,1)S(1)}, u32[]{:S(2)}, u32[]{:S(2)}) collective-permute-start(bf16[1,128,2048]{2,1,0:T(8,128)(2,1)S(1)} %collective-permute-done.4.refs_2_), channel_id=1, source_target_pairs={{0,16},{8,24},{16,0},{24,8},{1,17},{9,25},{17,1},{25,9},{2,18},{10... | collective-permute-start | bytes 1572872 | tf_op jit(solution)/shard_map/ppermute | solution.py:20
  100.2 24.6 %collective-permute-start.7 = (bf16[1,128,2048]{2,1,0:T(8,128)(2,1)S(1)}, bf16[1,128,2048]{2,1,0:T(8,128)(2,1)S(1)}, u32[]{:S(2)}, u32[]{:S(2)}) collective-permute-start(bf16[1,128,2048]{2,1,0:T(8,128)(2,1)S(1)} %collective-permute-done.3.refs_1_), channel_id=1, source_target_pairs={{0,16},{8,24},{16,0},{24,8},{1,17},{9,25},{17,1},{25,9},{2,18},{10... | collective-permute-start | bytes 1572872 | tf_op jit(solution)/shard_map/ppermute | solution.py:20
  124.8 1.0 copy-start.2
